TPU v7x, 32 devices: a whole 2x2x4 slice. The times are simulated.
32 devices in a mesh: pulse: 32 (over z, y, x, core), chan: 1.
Axes of the slice: x: 2, y: 2, z: 4, core: 2. Of those that a mesh axis runs over, the one named last changes fastest.
Arguments:
- echoes: bfloat16 [4, 128, 2, 5120], P('chan', 'pulse'), may hold values from -6 to 6
- replica: bfloat16 [2, 4096], replicated, may hold values from -0.0625 to 0.0625
- recon_filters: bfloat16 [4, 4, 2, 64], replicated, may hold values from -0.25 to 0.25
- span_offset: int32 [256], P('pulse'), may hold values from 0 to 4
- span_width: int32 [256], P('pulse'), may hold values from 1 to 4
- aperture_edges: int32 [2, 256], P(None, 'pulse'), may hold values from 0 to 16
Outputs:
- image: bfloat16 [4, 2, 256, 128], P(None, None, 'pulse', 'chan')
All inputs are finite; a program needn't handle non-finite values.
Results may differ from a plain program's by a relative error of at most 0.012.
Values may be sent and summed in bfloat16 or wider, within the bound.
A program may use at most 64 MiB of HBM per device.

v0:
```python
import functools

import jax
import jax.numpy as jnp
from jax import lax
from jax.experimental import pallas as pl
from jax.experimental.pallas import tpu as pltpu
from jax.sharding import PartitionSpec as P

LANES = 128
STEP = 4
BLOCK = LANES // STEP
NT = (((1,), (1,)), ((), ()))


def dot_nt(a, b):
    return lax.dot_general(a, b, NT, preferred_element_type=jnp.float32)


def range_rows(replica_ref, bmat_ref, bins, depth):
    span = 2 * bins
    windows = BLOCK // bins
    rows = BLOCK + bins
    taps = replica_ref.shape[1]
    replica = replica_ref[...].astype(jnp.float32)
    shifted = []
    for part in range(2):
        row = jnp.concatenate([replica[part : part + 1], jnp.zeros((1, depth - taps), jnp.float32)], axis=1)
        shifted.append(
            pltpu.roll(jnp.broadcast_to(row, (rows, depth)), 0, 1, stride=STEP, stride_axis=0)
        )
    real, imag = shifted
    half = windows * 2 * span
    for window in range(windows):
        low = window * bins
        real_part = real[low : low + span].astype(jnp.bfloat16)
        imag_part = imag[low : low + span].astype(jnp.bfloat16)
        at = window * 2 * span
        bmat_ref[at : at + span, :] = real_part
        bmat_ref[at + span : at + 2 * span, :] = imag_part
        bmat_ref[half + at : half + at + span, :] = -imag_part
        bmat_ref[half + at + span : half + at + 2 * span, :] = real_part


def azimuth_rows(filters_ref, tt_ref, step):
    samples, channels, _, taps = filters_ref.shape
    for s in range(samples):
        for c in range(channels):
            taps_row = filters_ref[s, c].astype(jnp.float32)
            taps_row = jnp.concatenate([taps_row, jnp.zeros((2, LANES - taps), jnp.float32)], axis=1)
            real, imag = [
                pltpu.roll(
                    jnp.broadcast_to(taps_row[part : part + 1], (step, LANES)), 0, 1, stride=1, stride_axis=0
                ).astype(jnp.bfloat16)
                for part in range(2)
            ]
            top, left = s * 2 * step, c * 2 * LANES
            tt_ref[top : top + step, left : left + LANES] = real
            tt_ref[top + step : top + 2 * step, left : left + LANES] = imag
            tt_ref[top : top + step, left + LANES : left + 2 * LANES] = -imag
            tt_ref[top + step : top + 2 * step, left + LANES : left + 2 * LANES] = real


def over_others(n):
    def run(step):
        if n <= 32:
            for k in range(1, n):
                step(k)
        else:
            pl.loop(1, n)(step)

    return run


def column(values, count):
    ids = lax.broadcasted_iota(jnp.int32, (count, LANES), 0)
    total = jnp.zeros((count, LANES), jnp.int32)
    for r in range(count):
        total = jnp.where(ids == r, values(r), total)
    return total


def kernel(
    n, whole_image,
    echoes_in, replica_in, filters_in, offset_in, width_in, edges_in,
    out_ref,
    replica_ref, filters_ref, offset_ref, width_ref, edges_ref,
    lines, bmat, tt, product, send, recv, turned,
    in_sem, send_sem, recv_sem,
):
    me = lax.axis_index("pulse")
    channels, pulses, _, samples = echoes_in.shape
    taps = replica_ref.shape[1]
    depth = bmat.shape[1]
    bin_count = (samples - taps) // STEP
    bins = bin_count // n
    span = 2 * bins
    windows = BLOCK // bins
    piece = 2 * span
    pairs = channels * pulses

    replica_fetch, echoes_fetch, *small_fetches = [
        pltpu.make_async_copy(source, held, in_sem.at[i])
        for i, (source, held) in enumerate(
            [
                (replica_in, replica_ref),
                (echoes_in.reshape(2 * channels * pulses, samples), lines.at[:, pl.ds(0, samples)]),
                (filters_in, filters_ref),
                (offset_in, offset_ref),
                (width_in, width_ref),
                (edges_in, edges_ref),
            ]
        )
    ]
    for fetch in [replica_fetch, echoes_fetch, *small_fetches]:
        fetch.start()

    barrier = pltpu.get_barrier_semaphore()

    @over_others(n)
    def _(k):
        pl.semaphore_signal(
            barrier, inc=1, device_id={"pulse": jnp.where(me + k < n, me + k, me + k - n)}, device_id_type=pl.DeviceIdType.MESH
        )

    replica_fetch.wait()
    range_rows(replica_ref, bmat, bins, depth)
    echoes_fetch.wait()
    lines[:, samples:] = jnp.zeros((2 * pairs, lines.shape[1] - samples), lines.dtype)

    blocks = bin_count // BLOCK
    group = min(blocks, 8)
    rows = 2 * pulses
    lane = lax.broadcasted_iota(jnp.int32, (group * pulses, LANES), 1)
    for first in range(0, blocks, group):
        rows_in = jnp.concatenate(
            [lines[:, LANES * a : LANES * a + depth] for a in range(first, first + group)], axis=0
        )
        result = dot_nt(rows_in, bmat[...])
        for a in range(group):
            for c in range(channels):
                at = (a * channels + c) * rows
                for half in range(2):
                    product[half, c, a * rows : (a + 1) * rows, :] = result[
                        at : at + rows, half * LANES : (half + 1) * LANES
                    ]
        by_channel = [
            product[0, c, pl.ds(0, group * pulses, stride=2), :]
            + product[1, c, pl.ds(1, group * pulses, stride=2), :]
            for c in range(channels)
        ]
        for w in range(windows):
            message = None
            for c in range(channels):
                shift = (piece * (c - w)) % LANES
                moved = pltpu.roll(by_channel[c], shift, 1) if shift else by_channel[c]
                message = moved if c == 0 else jnp.where(lane >= piece * c, moved, message)
            for a in range(group):
                send[(first + a) * windows + w] = message[a * pulses : (a + 1) * pulses].astype(send.dtype)

    pl.semaphore_wait(barrier, n - 1)

    @over_others(n)
    def _(k):
        to = jnp.where(me + k < n, me + k, me + k - n)
        pltpu.make_async_remote_copy(
            src_ref=send.at[to], dst_ref=recv.at[me], send_sem=send_sem, recv_sem=recv_sem,
            device_id={"pulse": to}, device_id_type=pl.DeviceIdType.MESH,
        ).start()

    recv[me] = send[me]

    for fetch in small_fetches:
        fetch.wait()
    all_pulses = n * pulses
    row_id = lax.broadcasted_iota(jnp.int32, (bins, LANES), 0)
    lane_id = lax.broadcasted_iota(jnp.int32, (bins, LANES), 1)
    first_bin = row_id + column(lambda r: offset_ref[r], bins)
    width = column(lambda r: width_ref[r], bins)
    low_edge = column(lambda r: edges_ref[0, r], bins)
    high_edge = all_pulses - column(lambda r: edges_ref[1, r], bins)
    place = lane_id % span
    chosen = (place >= first_bin) & (place < first_bin + width) & (place + me * bins < bin_count)
    select = jnp.concatenate(
        [
            jnp.where(chosen & (lane_id // span == g), 1.0, 0.0)
            for g in range(2 * channels)
        ],
        axis=0,
    ).astype(jnp.bfloat16)
    scale = 1.0 / width.astype(jnp.float32)

    margin = (turned.shape[0] - all_pulses) // 2
    if whole_image:
        turned[0:margin, :] = jnp.zeros((margin, LANES), jnp.float32)
        turned[margin + all_pulses :, :] = jnp.zeros((margin, LANES), jnp.float32)
        azimuth_rows(filters_ref, tt, tt.shape[0] // (2 * filters_ref.shape[0]))

    pltpu.make_async_copy(send.at[pl.ds(0, n - 1)], recv.at[pl.ds(0, n - 1)], recv_sem).wait()

    for i in range(n):
        turned[margin + i * pulses : margin + (i + 1) * pulses, :] = recv[i].astype(jnp.float32)

    def corrected(start):
        taken = dot_nt(select, turned[start : start + LANES, :].astype(jnp.bfloat16))
        pulse = lane_id + (start - margin)
        weight = jnp.where((pulse >= low_edge) & (pulse < high_edge), scale, 0.0)
        return [taken[g * bins : (g + 1) * bins] * weight for g in range(2 * channels)]

    if whole_image:
        samples_out = filters_ref.shape[0]
        step = LANES // 2
        rows_in = jnp.concatenate(
            [jnp.concatenate(corrected(start), axis=1) for start in range(0, all_pulses, step)], axis=0
        ).astype(jnp.bfloat16)
        image = dot_nt(rows_in, tt[...])
        left = lane_id < step
        for s in range(samples_out):
            for b in range(all_pulses // LANES):
                at = 2 * b * bins
                early = image[at : at + bins, s * LANES : (s + 1) * LANES]
                late = image[at + bins : at + 2 * bins, s * LANES : (s + 1) * LANES]
                real = jnp.where(left, early, pltpu.roll(late, step, 1))
                imag = jnp.where(left, pltpu.roll(early, step, 1), late)
                out_ref[s, 0, :, b * LANES : (b + 1) * LANES] = real.astype(out_ref.dtype)
                out_ref[s, 1, :, b * LANES : (b + 1) * LANES] = imag.astype(out_ref.dtype)
    else:
        for b in range(all_pulses // LANES):
            for g, part in enumerate(corrected(b * LANES)):
                out_ref[g // 2, g % 2, :, b * LANES : (b + 1) * LANES] = part.astype(out_ref.dtype)

    pltpu.make_async_copy(send.at[pl.ds(0, n - 1)], recv.at[pl.ds(0, n - 1)], send_sem).wait()


def run_kernel(echoes, replica, recon_filters, span_offset, span_width, aperture_edges, whole_image):
    n = lax.axis_size("pulse")
    channels, pulses, _, samples = echoes.shape
    taps = replica.shape[1]
    bin_count = (samples - taps) // STEP
    bins = bin_count // n
    span = 2 * bins
    all_pulses = n * pulses
    blocks = bin_count // BLOCK
    group = min(blocks, 8)
    assert BLOCK % bins == 0 and channels * 2 * span == LANES and channels == BLOCK // bins
    assert blocks % group == 0 and all_pulses % LANES == 0
    depth = taps + 2 * LANES
    samples_out, _, _, az_taps = recon_filters.shape
    step = LANES // 2
    assert az_taps == step
    if whole_image:
        margin = az_taps // 2
        out_shape = (samples_out, 2, bins, all_pulses)
        tt_shape = (samples_out * 2 * step, channels * 2 * LANES)
    else:
        margin = 0
        out_shape = (channels, 2, bins, all_pulses)
        tt_shape = (16, LANES)
    operands = [
        pltpu.with_memory_space_constraint(array, pltpu.HBM)
        for array in (echoes, replica, recon_filters, span_offset, span_width, aperture_edges)
    ]
    vmem = pl.BlockSpec(memory_space=pltpu.VMEM)
    return pl.pallas_call(
        functools.partial(kernel, n, whole_image),
        out_shape=jax.ShapeDtypeStruct(out_shape, jnp.bfloat16),
        in_specs=[pl.BlockSpec(memory_space=pltpu.HBM)] * 6,
        out_specs=vmem,
        scratch_shapes=[
            pltpu.VMEM(replica.shape, jnp.bfloat16),
            pltpu.VMEM(recon_filters.shape, jnp.bfloat16),
            pltpu.SMEM(span_offset.shape, jnp.int32),
            pltpu.SMEM(span_width.shape, jnp.int32),
            pltpu.SMEM(aperture_edges.shape, jnp.int32),
            pltpu.VMEM((2 * channels * pulses, samples + LANES), jnp.bfloat16),
            pltpu.VMEM((2 * LANES, depth), jnp.bfloat16),
            pltpu.VMEM(tt_shape, jnp.bfloat16),
            pltpu.VMEM((2, channels, group * 2 * pulses, LANES), jnp.float32),
            pltpu.VMEM((n, pulses, LANES), jnp.bfloat16),
            pltpu.VMEM((n, pulses, LANES), jnp.bfloat16),
            pltpu.VMEM((all_pulses + 2 * margin, LANES), jnp.float32),
            pltpu.SemaphoreType.DMA((6,)),
            pltpu.SemaphoreType.DMA,
            pltpu.SemaphoreType.DMA,
        ],
        compiler_params=pltpu.CompilerParams(
            collective_id=0, has_side_effects=True, vmem_limit_bytes=32 * 1024 * 1024
        ),
    )(*operands)


def with_neighbours(cells, axis, dim, width):
    count = lax.axis_size(axis)
    head = lax.slice_in_dim(cells, 0, width, axis=dim)
    tail = lax.slice_in_dim(cells, cells.shape[dim] - width, cells.shape[dim], axis=dim)
    up = [(i, i + 1) for i in range(count - 1)]
    down = [(i + 1, i) for i in range(count - 1)]
    return jnp.concatenate(
        [lax.ppermute(tail, axis, up), cells, lax.ppermute(head, axis, down)], axis=dim
    )


def azimuth(padded, filters):
    channels, _, bin_count, padded_len = padded.shape
    subbands = filters.shape[0]
    tap_count = filters.shape[3]
    pulses = padded_len - tap_count
    span_len = tap_count + 4
    step_count = span_len // 4
    quartets = padded.reshape(channels, 2, bin_count, padded_len // 4, 4)
    window = jnp.stack(
        [quartets[:, :, :, first : first + pulses // 4, :] for first in range(step_count)], 4
    )
    window = window.transpose(2, 3, 0, 1, 4, 5).reshape(
        bin_count * (pulses // 4), channels * 2 * span_len
    )
    offset = jnp.arange(span_len)[:, None] - jnp.arange(4)[None, :]
    inside = (offset >= 0) & (offset < tap_count)
    picked = jnp.where(inside, jnp.take(filters, jnp.clip(offset, 0, tap_count - 1), axis=3), 0)
    real, imag = picked[:, :, 0], picked[:, :, 1]
    matrix = jnp.stack([jnp.stack([real, imag], 3), jnp.stack([-imag, real], 3)], 2)
    matrix = matrix.transpose(1, 2, 3, 0, 4, 5).reshape(channels * 2 * span_len, subbands * 8)
    result = jnp.dot(window, matrix, preferred_element_type=jnp.float32)
    result = result.reshape(bin_count, pulses // 4, subbands, 2, 4).transpose(2, 3, 0, 1, 4)
    return result.reshape(subbands, 2, bin_count, pulses)


def body(echoes, replica, recon_filters, span_offset, span_width, aperture_edges):
    operands = (echoes, replica, recon_filters, span_offset, span_width, aperture_edges)
    if lax.axis_size("chan") == 1 and echoes.shape[0] == recon_filters.shape[1]:
        return run_kernel(*operands, whole_image=True)
    corrected = run_kernel(*operands, whole_image=False)
    corrected = lax.all_to_all(corrected, "chan", split_axis=3, concat_axis=0, tiled=True)
    padded = with_neighbours(corrected, "chan", 3, recon_filters.shape[3] // 2)
    return azimuth(padded, recon_filters).astype(jnp.bfloat16)


def solution(mesh):
    return jax.shard_map(
        body,
        mesh=mesh,
        in_specs=(
            P("chan", "pulse", None, None),
            P(),
            P(),
            P("pulse"),
            P("pulse"),
            P(None, "pulse"),
        ),
        out_specs=P(None, None, "pulse", "chan"),
        check_vma=False,
    )
```

profile of v0, /device:TPU:0, one launch (start us, length us, event | category | flops | bytes accessed | tf_op | source)
XLA Modules:
  0.0 12.2 jit_solution(5152418097512023181)
XLA Ops:
  0.0 11.5 %shard_map.64 = bf16[4,2,8,128]{3,2,1,0:T(8,128)(2,1)S(1)} custom-call(bf16[4,4,2,5120]{3,2,1,0:T(2,128)(2,1)} %echoes_in.1, bf16[2,4096]{1,0:T(2,128)(2,1)} %replica_in.1, bf16[4,4,2,64]{3,2,1,0:T(2,128)(2,1)} %filters_in.1, s32[8]{0:T(128)} %offset_in.1, s32[8]{0:T(128)} %width_in.1, s32[2,8]{1,0:T(2,128)} %edges_in.1), custom_call_target="tpu_custom_call" | custom-call | tf_op jit(solution)/shard_map/pallas_call | solution.py:264
  11.5 0.6 %copy.8 = bf16[4,2,8,128]{3,2,1,0:T(8,128)(2,1)} copy(bf16[4,2,8,128]{3,2,1,0:T(8,128)(2,1)S(1)} %shard_map.64) | data formatting | bytes 32768
where the time goes:
time: 12.4 us; the launch traced here: 12.2 us
  Pallas kernels  11.5 us (93%)
  local copies, waits for them, and re-layouts  0.61 us (5%)
    pallas_call x1, Pallas kernels, run_kernel(): pl.pallas_call(functools.partial(kernel, n, whole_image), out_shape=jax.S...  11.5 us
    unnamed x1, local copies, waits for them, and re-layouts  0.61 us

commit v1 on v0

--- a/solution.py
+++ b/solution.py
@@ -17,29 +17,16 @@
     return lax.dot_general(a, b, NT, preferred_element_type=jnp.float32)
 
 
-def range_rows(replica_ref, bmat_ref, bins, depth):
-    span = 2 * bins
-    windows = BLOCK // bins
-    rows = BLOCK + bins
+def range_rows(replica_ref, bmat_ref, rows, depth):
     taps = replica_ref.shape[1]
+    half = bmat_ref.shape[0] // 2
+    filled = -(-rows // 16) * 16
     replica = replica_ref[...].astype(jnp.float32)
-    shifted = []
     for part in range(2):
         row = jnp.concatenate([replica[part : part + 1], jnp.zeros((1, depth - taps), jnp.float32)], axis=1)
-        shifted.append(
-            pltpu.roll(jnp.broadcast_to(row, (rows, depth)), 0, 1, stride=STEP, stride_axis=0)
-        )
-    real, imag = shifted
-    half = windows * 2 * span
-    for window in range(windows):
-        low = window * bins
-        real_part = real[low : low + span].astype(jnp.bfloat16)
-        imag_part = imag[low : low + span].astype(jnp.bfloat16)
-        at = window * 2 * span
-        bmat_ref[at : at + span, :] = real_part
-        bmat_ref[at + span : at + 2 * span, :] = imag_part
-        bmat_ref[half + at : half + at + span, :] = -imag_part
-        bmat_ref[half + at + span : half + at + 2 * span, :] = real_part
+        shifted = pltpu.roll(jnp.broadcast_to(row, (rows, depth)), 0, 1, stride=STEP, stride_axis=0)
+        shifted = jnp.concatenate([shifted, jnp.zeros((filled - rows, depth), jnp.float32)], axis=0)
+        bmat_ref[part * half : part * half + filled, :] = shifted.astype(jnp.bfloat16)
 
 
 def azimuth_rows(filters_ref, tt_ref, step):
@@ -96,15 +83,20 @@
     bins = bin_count // n
     span = 2 * bins
     windows = BLOCK // bins
-    piece = 2 * span
     pairs = channels * pulses
 
-    replica_fetch, echoes_fetch, *small_fetches = [
+    echo_rows = echoes_in.reshape(2 * pairs, samples)
+    quarter = samples // 4
+    quarters = [pl.ds(i * quarter, quarter) for i in range(4)]
+    echoes_fetches = [
+        pltpu.make_async_copy(echo_rows.at[:, at], lines.at[:, at], in_sem.at[5 + i])
+        for i, at in enumerate(quarters)
+    ]
+    replica_fetch, *small_fetches = [
         pltpu.make_async_copy(source, held, in_sem.at[i])
         for i, (source, held) in enumerate(
             [
                 (replica_in, replica_ref),
-                (echoes_in.reshape(2 * channels * pulses, samples), lines.at[:, pl.ds(0, samples)]),
                 (filters_in, filters_ref),
                 (offset_in, offset_ref),
                 (width_in, width_ref),
@@ -112,7 +104,7 @@
             ]
         )
     ]
-    for fetch in [replica_fetch, echoes_fetch, *small_fetches]:
+    for fetch in [replica_fetch, *echoes_fetches, *small_fetches]:
         fetch.start()
 
     barrier = pltpu.get_barrier_semaphore()
@@ -123,10 +115,14 @@
             barrier, inc=1, device_id={"pulse": jnp.where(me + k < n, me + k, me + k - n)}, device_id_type=pl.DeviceIdType.MESH
         )
 
+    lines[:, samples:] = jnp.zeros((2 * pairs, lines.shape[1] - samples), lines.dtype)
+    half = LANES // 2
+    for part in range(2):
+        bmat[(part + 1) * half - 16 : (part + 1) * half, :] = jnp.zeros((16, depth), bmat.dtype)
     replica_fetch.wait()
-    range_rows(replica_ref, bmat, bins, depth)
-    echoes_fetch.wait()
-    lines[:, samples:] = jnp.zeros((2 * pairs, lines.shape[1] - samples), lines.dtype)
+    range_rows(replica_ref, bmat, BLOCK + bins, depth)
+    for fetch in echoes_fetches:
+        fetch.wait()
 
     blocks = bin_count // BLOCK
     group = min(blocks, 8)
@@ -140,21 +136,18 @@
         for a in range(group):
             for c in range(channels):
                 at = (a * channels + c) * rows
-                for half in range(2):
-                    product[half, c, a * rows : (a + 1) * rows, :] = result[
-                        at : at + rows, half * LANES : (half + 1) * LANES
-                    ]
-        by_channel = [
-            product[0, c, pl.ds(0, group * pulses, stride=2), :]
-            + product[1, c, pl.ds(1, group * pulses, stride=2), :]
-            for c in range(channels)
-        ]
+                product[c, a * rows : (a + 1) * rows, :] = result[at : at + rows]
+        by_channel = []
+        for c in range(channels):
+            from_real = product[c, pl.ds(0, group * pulses, stride=2), :]
+            from_imag = pltpu.roll(product[c, pl.ds(1, group * pulses, stride=2), :], half, 1)
+            by_channel.append(jnp.where(lane < half, from_real - from_imag, from_real + from_imag))
         for w in range(windows):
             message = None
             for c in range(channels):
-                shift = (piece * (c - w)) % LANES
+                shift = (span * c - bins * w) % LANES
                 moved = pltpu.roll(by_channel[c], shift, 1) if shift else by_channel[c]
-                message = moved if c == 0 else jnp.where(lane >= piece * c, moved, message)
+                message = moved if c == 0 else jnp.where(lane % half >= span * c, moved, message)
             for a in range(group):
                 send[(first + a) * windows + w] = message[a * pulses : (a + 1) * pulses].astype(send.dtype)
 
@@ -183,18 +176,21 @@
     chosen = (place >= first_bin) & (place < first_bin + width) & (place + me * bins < bin_count)
     select = jnp.concatenate(
         [
-            jnp.where(chosen & (lane_id // span == g), 1.0, 0.0)
+            jnp.where(chosen & (lane_id // span == g % 2 * channels + g // 2), 1.0, 0.0)
             for g in range(2 * channels)
         ],
         axis=0,
     ).astype(jnp.bfloat16)
     scale = 1.0 / width.astype(jnp.float32)
 
-    margin = (turned.shape[0] - all_pulses) // 2
+    samples_out, _, _, az_taps = filters_ref.shape
+    margin = az_taps // 2 if whole_image else 0
     if whole_image:
+        step = tt.shape[0] // (2 * samples_out)
+        after = turned.shape[0] - margin - all_pulses
         turned[0:margin, :] = jnp.zeros((margin, LANES), jnp.float32)
-        turned[margin + all_pulses :, :] = jnp.zeros((margin, LANES), jnp.float32)
-        azimuth_rows(filters_ref, tt, tt.shape[0] // (2 * filters_ref.shape[0]))
+        turned[margin + all_pulses :, :] = jnp.zeros((after, LANES), jnp.float32)
+        azimuth_rows(filters_ref, tt, step)
 
     pltpu.make_async_copy(send.at[pl.ds(0, n - 1)], recv.at[pl.ds(0, n - 1)], recv_sem).wait()
 
@@ -208,22 +204,22 @@
         return [taken[g * bins : (g + 1) * bins] * weight for g in range(2 * channels)]
 
     if whole_image:
-        samples_out = filters_ref.shape[0]
-        step = LANES // 2
         rows_in = jnp.concatenate(
             [jnp.concatenate(corrected(start), axis=1) for start in range(0, all_pulses, step)], axis=0
         ).astype(jnp.bfloat16)
         image = dot_nt(rows_in, tt[...])
-        left = lane_id < step
-        for s in range(samples_out):
+        share = LANES // step
+        for o in range(2 * samples_out):
+            tile, at = o // share, o % share
             for b in range(all_pulses // LANES):
-                at = 2 * b * bins
-                early = image[at : at + bins, s * LANES : (s + 1) * LANES]
-                late = image[at + bins : at + 2 * bins, s * LANES : (s + 1) * LANES]
-                real = jnp.where(left, early, pltpu.roll(late, step, 1))
-                imag = jnp.where(left, pltpu.roll(early, step, 1), late)
-                out_ref[s, 0, :, b * LANES : (b + 1) * LANES] = real.astype(out_ref.dtype)
-                out_ref[s, 1, :, b * LANES : (b + 1) * LANES] = imag.astype(out_ref.dtype)
+                joined = None
+                for i in range(share):
+                    top = (b * share + i) * bins
+                    part = image[top : top + bins, tile * LANES : (tile + 1) * LANES]
+                    shift = (i - at) * step % LANES
+                    part = pltpu.roll(part, shift, 1) if shift else part
+                    joined = part if i == 0 else jnp.where(lane_id >= i * step, part, joined)
+                out_ref[o // 2, o % 2, :, b * LANES : (b + 1) * LANES] = joined.astype(out_ref.dtype)
     else:
         for b in range(all_pulses // LANES):
             for g, part in enumerate(corrected(b * LANES)):
@@ -242,18 +238,19 @@
     all_pulses = n * pulses
     blocks = bin_count // BLOCK
     group = min(blocks, 8)
-    assert BLOCK % bins == 0 and channels * 2 * span == LANES and channels == BLOCK // bins
+    assert BLOCK % bins == 0 and channels * 2 * span == LANES
+    assert BLOCK + bins <= LANES // 2 and samples % (4 * LANES) == 0
     assert blocks % group == 0 and all_pulses % LANES == 0
     depth = taps + 2 * LANES
     samples_out, _, _, az_taps = recon_filters.shape
-    step = LANES // 2
-    assert az_taps == step
+    step = az_taps // 2
+    assert az_taps + step <= LANES
     if whole_image:
-        margin = az_taps // 2
+        turned_rows = all_pulses - step + LANES
         out_shape = (samples_out, 2, bins, all_pulses)
         tt_shape = (samples_out * 2 * step, channels * 2 * LANES)
     else:
-        margin = 0
+        turned_rows = all_pulses
         out_shape = (channels, 2, bins, all_pulses)
         tt_shape = (16, LANES)
     operands = [
@@ -273,13 +270,13 @@
             pltpu.SMEM(span_width.shape, jnp.int32),
             pltpu.SMEM(aperture_edges.shape, jnp.int32),
             pltpu.VMEM((2 * channels * pulses, samples + LANES), jnp.bfloat16),
-            pltpu.VMEM((2 * LANES, depth), jnp.bfloat16),
+            pltpu.VMEM((LANES, depth), jnp.bfloat16),
             pltpu.VMEM(tt_shape, jnp.bfloat16),
-            pltpu.VMEM((2, channels, group * 2 * pulses, LANES), jnp.float32),
+            pltpu.VMEM((channels, group * 2 * pulses, LANES), jnp.float32),
             pltpu.VMEM((n, pulses, LANES), jnp.bfloat16),
             pltpu.VMEM((n, pulses, LANES), jnp.bfloat16),
-            pltpu.VMEM((all_pulses + 2 * margin, LANES), jnp.float32),
-            pltpu.SemaphoreType.DMA((6,)),
+            pltpu.VMEM((turned_rows, LANES), jnp.float32),
+            pltpu.SemaphoreType.DMA((9,)),
             pltpu.SemaphoreType.DMA,
             pltpu.SemaphoreType.DMA,
         ],

time: 12.4 us -> 12.2 us (0.984)
  Pallas kernels: 11.5 us -> 11.3 us
    pallas_call x1, Pallas kernels: 11.5 us -> 11.3 us  [run_kernel(): pl.pallas_call(functools.partial(kernel, n, whole_image), out_shape=jax.S...]
where the time goes in v1:
time: 12.2 us; the launch traced here: 11.9 us
  Pallas kernels  11.3 us (93%)
  local copies, waits for them, and re-layouts  0.61 us (5%)
    pallas_call x1, Pallas kernels, run_kernel(): pl.pallas_call(functools.partial(kernel, n, whole_image), out_shape=jax.S...  11.3 us
    unnamed x1, local copies, waits for them, and re-layouts  0.61 us

profile of v1, /device:TPU:0, one launch (start us, length us, event | category | flops | bytes accessed | tf_op | source)
XLA Modules:
  0.0 11.9 jit_solution(16018653877729728936)
XLA Ops:
  0.0 11.3 %shard_map.64 = bf16[4,2,8,128]{3,2,1,0:T(8,128)(2,1)S(1)} custom-call(bf16[4,4,2,5120]{3,2,1,0:T(2,128)(2,1)} %echoes_in.1, bf16[2,4096]{1,0:T(2,128)(2,1)} %replica_in.1, bf16[4,4,2,64]{3,2,1,0:T(2,128)(2,1)} %filters_in.1, s32[8]{0:T(128)} %offset_in.1, s32[8]{0:T(128)} %width_in.1, s32[2,8]{1,0:T(2,128)} %edges_in.1), custom_call_target="tpu_custom_call" | custom-call | tf_op jit(solution)/shard_map/pallas_call | solution.py:261
  11.3 0.6 %copy.8 = bf16[4,2,8,128]{3,2,1,0:T(8,128)(2,1)} copy(bf16[4,2,8,128]{3,2,1,0:T(8,128)(2,1)S(1)} %shard_map.64) | data formatting | bytes 32768
